TPU v7x, 32 devices: a whole 2x2x4 slice. The times are simulated.
32 devices in a mesh: dom: 4 (over y, core), aux: 8 (over z, x).
Axes of the slice: x: 2, y: 2, z: 4, core: 2. Of those that a mesh axis runs over, the one named last changes fastest.
Arguments:
- integrals: bfloat16 [4, 1024, 512, 128], P('dom', 'aux'), may hold values from -0.25 to 0.25
- density: bfloat16 [4, 4, 128, 128], P('dom'), may hold values from -0.25 to 0.25
- dens_cols: int32 [4, 4], replicated, may hold values from 0 to 3, as said below
- neighbours: int32 [4, 4], replicated, may hold values from 0 to 3, as said below
- metric: bfloat16 [4, 1024, 1024], P('dom', 'aux'), may hold values from -0.5 to 2.5, as said below
Outputs:
- exchange: float32 [4, 128, 128], P('dom')
Inputs may be any that keep to these rules, and one draw needn't show every extreme that they name: `neighbours`: in each row the entries are distinct; position 0 holds the row's own block, the others are blocks within cyclic distance 2 of it, both blocks at distance 1 among them. `dens_cols`: in each row the entries are distinct; position 0 holds the row's own block, the others are blocks within cyclic distance 2 of it, both blocks at distance 1 among them. `metric`: each domain's matrix is symmetric.
All inputs are finite; a program needn't handle non-finite values.
Results may differ from a plain program's by a relative error of at most 0.004.
Values may be sent and summed in bfloat16 or wider, within the bound.
A program may use at most 128 MiB of HBM per device.

v0:
```python
import jax
import jax.numpy as jnp
from jax import lax
from jax.sharding import PartitionSpec as P

RAD = 2


def passed_along(block, axis, distance):
    devices = range(lax.axis_size(axis))
    route = [((i - distance) % len(devices), i) for i in devices]
    return lax.ppermute(block, axis, route)


def body(integrals, density, dens_cols, neighbours, metric):
    domain_count = lax.axis_size("dom")
    my_domain = lax.axis_index("dom")
    block_size = density.shape[2]
    neigh_count = neighbours.shape[1]
    my_blocks = lax.dynamic_index_in_dim(neighbours, my_domain, 0, keepdims=False)
    slab_list = []
    for offset in range(-RAD, RAD + 1):
        if offset == 0:
            slab_list.append(density[0])
        else:
            slab_list.append(passed_along(density, "dom", -offset)[0])
    row_slabs = jnp.stack(slab_list)
    slot_index = (my_blocks - my_domain + RAD) % domain_count
    picked = jnp.take(row_slabs, slot_index, axis=0)
    tile_cols = jnp.take(dens_cols, my_blocks, axis=0)
    matches = (tile_cols[:, None, :] == my_blocks[None, :, None]).astype(jnp.bfloat16)
    dense_tiles = jnp.einsum("jsk,jkab->jasb", matches, picked, preferred_element_type=jnp.float32)
    density_local = dense_tiles.astype(jnp.bfloat16).reshape(
        neigh_count * block_size, neigh_count * block_size
    )
    half_product = jnp.einsum(
        "ls,plm->psm", density_local, integrals[0], preferred_element_type=jnp.float32
    ).astype(jnp.bfloat16)
    half_moved, ints_moved = (
        lax.all_to_all(half_product[None], "aux", split_axis=2, concat_axis=1, tiled=True),
        lax.all_to_all(integrals, "aux", split_axis=2, concat_axis=1, tiled=True),
    )
    columns = ints_moved[0].reshape(ints_moved.shape[1], -1)
    fitted = jnp.dot(
        lax.all_gather(metric, "aux", axis=1, tiled=True)[0],
        columns,
        preferred_element_type=jnp.float32,
    ).astype(jnp.bfloat16)
    fitted = fitted.reshape(half_moved.shape[1:])
    partial_value = jnp.einsum(
        "psm,psn->mn", half_moved[0], fitted, preferred_element_type=jnp.float32
    )
    summed = lax.psum(partial_value, "aux")
    return summed[None]


def solution(mesh):
    return jax.shard_map(
        body,
        mesh=mesh,
        in_specs=(
            P("dom", "aux", None, None),
            P("dom", None, None, None),
            P(),
            P(),
            P("dom", "aux", None),
        ),
        out_specs=P("dom", None, None),
        check_vma=False,
    )
```

profile of v0, /device:TPU:0, one launch (start us, length us, event | category | flops | bytes accessed | tf_op | source)
XLA Modules:
  0.0 929.4 jit_solution(7285030264542253923)
XLA Ops:
  6.5 0.0 copy-start
  6.5 18.6 %copy.19 = bf16[1,128,512,128]{3,1,0,2:T(8,128)(2,1)} copy(bf16[1,128,512,128]{3,2,1,0:T(8,128)(2,1)} %param.5) | data formatting | bytes 33554432 | tf_op args[0]
  25.2 0.0 copy-start.2
  25.2 7.4 all-to-all-start.1
  32.5 0.0 copy-done.2
  32.5 1.6 collective-permute-start
  34.1 0.0 collective-permute-start.1
  34.1 1.7 collective-permute-start.2
  35.9 0.7 compare_and_fusion
  36.6 0.0 copy-done
  36.6 0.6 gather_fusion.1
  37.2 0.1 broadcast_select_fusion.1
  37.3 0.8 collective-permute-done
  38.1 1.9 collective-permute-done.1
  40.0 0.0 collective-permute-done.2
  40.0 0.6 gather_fusion
  40.7 0.1 broadcast_select_fusion
  40.8 0.5 convolution_convert_fusion
  41.4 18.2 %convert_bitcast_fusion.1 = bf16[1,128,512,128]{3,2,1,0:T(8,128)(2,1)} fusion(bf16[1,128,512,128]{3,2,1,0:T(8,128)(2,1)} %param.5, bf16[64,8,4,128]{3,2,1,0:T(4,128)(2,1)S(1)} %bitcast.69), kind=kOutput, calls=%fused_computation.11 | convolution fusion | flops 8598323200 | bytes 34078720 | tf_op jit(solution)/shard_map/ls,plm->psm/dot_general | solution.py:36
  59.6 18.6 %copy.17 = bf16[1,128,512,128]{3,1,0,2:T(8,128)(2,1)} copy(bf16[1,128,512,128]{3,2,1,0:T(8,128)(2,1)} %convert_bitcast_fusion.1) | data formatting | bytes 33554432 | tf_op jit(solution)/shard_map/broadcast_in_dim | solution.py:40
  78.2 317.5 %all-to-all-done.1 = bf16[1,128,512,128]{3,1,0,2:T(8,128)(2,1)} async-done(((bf16[1,128,512,128]{3,1,0,2:T(8,128)(2,1)}), bf16[1,128,512,128]{3,1,0,2:T(8,128)(2,1)}, u32[]{:S(2)}, u32[]{:S(2)}) %all-to-all-start.1) | async-done | bytes 16777248 | tf_op jit(solution)/shard_map/all_to_all | solution.py:41
  395.6 5.7 all-to-all-start
  401.4 0.0 all-gather.2.cloned.1.call-start
  401.4 0.7 all-gather.2.cloned.1.call-update
  402.1 0.0 all-reduce.2.cloned.1.call-start
  402.2 18.6 %copy.20 = bf16[1,128,8,64,128]{4,3,1,2,0:T(8,128)(2,1)} copy(bf16[1,128,8,64,128]{4,1,3,2,0:T(8,128)(2,1)} %bitcast.14) | data formatting | bytes 33554432 | tf_op jit(solution)/shard_map/all_to_all | solution.py:41
  420.7 288.2 %all-gather.2.cloned.1.call-done = bf16[1,1024,1024]{2,1,0:T(8,128)(2,1)} async-done(((bf16[1,128,1024]{2,1,0:T(8,128)(2,1)}), bf16[1,1024,1024]{2,1,0:T(8,128)(2,1)}) %all-gather.2.cloned.1.call-update) | async-done | bytes 2097168 | tf_op jit(solution)/shard_map/all_gather | solution.py:45
  708.9 43.8 %convert_bitcast_fusion = bf16[128,64,8,128]{3,2,1,0:T(8,128)(2,1)} fusion(bf16[128,8,64,128]{3,2,1,0:T(8,128)(2,1)} %bitcast.67, bf16[1,1024,1024]{2,1,0:T(8,128)(2,1)} %all-gather.2.cloned.1.call-done), kind=kOutput, calls=%fused_computation.10 | convolution fusion | flops 17188257792 | bytes 35651584 | tf_op jit(solution)/shard_map/dot_general | solution.py:44
  752.7 36.0 %all-to-all-done = bf16[1,128,512,128]{3,1,0,2:T(8,128)(2,1)} async-done(((bf16[1,128,512,128]{3,1,0,2:T(8,128)(2,1)}), bf16[1,128,512,128]{3,1,0,2:T(8,128)(2,1)}, u32[]{:S(2)}, u32[]{:S(2)}) %all-to-all-start) | async-done | bytes 16777248 | tf_op jit(solution)/shard_map/all_to_all | solution.py:40
  788.7 23.3 %copy.18 = bf16[1,128,8,64,128]{1,2,4,3,0:T(8,128)(2,1)} copy(bf16[1,128,8,64,128]{4,1,3,2,0:T(8,128)(2,1)} %bitcast.11) | data formatting | bytes 33554432 | tf_op jit(solution)/shard_map/all_to_all | solution.py:40
  812.0 0.0 copy-start.1
  812.0 25.3 %squeeze.18 = bf16[1024,64,128]{0,2,1:T(8,128)(2,1)} reshape(bf16[1,8,128,64,128]{2,1,4,3,0:T(8,128)(2,1)} %bitcast.66) | data formatting | bytes 33554432 | tf_op jit(solution)/shard_map/squeeze | solution.py:51
  837.3 16.2 %fusion.13 = f32[1,128,128]{2,1,0:T(8,128)} fusion(bf16[1024,64,128]{0,2,1:T(8,128)(2,1)} %squeeze.18, bf16[128,64,8,128]{3,2,1,0:T(8,128)(2,1)} %convert_bitcast_fusion), kind=kOutput, calls=%fused_computation.14 | convolution fusion | flops 2147483648 | bytes 33619968 | tf_op jit(solution)/shard_map/psm,psn->mn/dot_general | solution.py:50
  853.5 0.0 all-reduce.2.cloned.1.call-update
  853.5 67.6 %all-reduce.2.cloned.1.call-done = f32[1,128,128]{2,1,0:T(8,128)} async-done(((f32[1,128,128]{2,1,0:T(8,128)}), f32[1,128,128]{2,1,0:T(8,128)}) %all-reduce.2.cloned.1.call-update) | async-done | bytes 65552 | tf_op jit(solution)/shard_map/psum | solution.py:53
  921.1 1.5 copy.51
  922.6 0.0 copy-done.1
  (9 shorter events, 0.1 us)
Async XLA Ops:
  6.5 30.1 %copy-start = (s32[4,4]{1,0:T(4,128)S(1)}, s32[4,4]{1,0:T(4,128)}, u32[]{:S(2)}) copy-start(s32[4,4]{1,0:T(4,128)} %param.7) | copy-start | bytes 196
  25.2 7.4 copy-start.2
  25.2 370.5 %all-to-all-start.1 = ((bf16[1,128,512,128]{3,1,0,2:T(8,128)(2,1)}), bf16[1,128,512,128]{3,1,0,2:T(8,128)(2,1)}, u32[]{:S(2)}, u32[]{:S(2)}) async-start(bf16[1,128,512,128]{3,1,0,2:T(8,128)(2,1)} %copy.19), calls=%async_computation.1 | async-start | bytes 33554432 | tf_op jit(solution)/shard_map/all_to_all | solution.py:41
  32.5 5.5 collective-permute-start
  34.1 5.8 collective-permute-start.1
  34.1 5.8 collective-permute-start.2
  395.6 393.1 %all-to-all-start = ((bf16[1,128,512,128]{3,1,0,2:T(8,128)(2,1)}), bf16[1,128,512,128]{3,1,0,2:T(8,128)(2,1)}, u32[]{:S(2)}, u32[]{:S(2)}) async-start(bf16[1,128,512,128]{3,1,0,2:T(8,128)(2,1)} %copy.17), calls=%async_computation | async-start | bytes 33554432 | tf_op jit(solution)/shard_map/all_to_all | solution.py:40
  401.4 307.5 %all-gather.2.cloned.1.call-start = ((), (), s32[]{:S(2)}) async-start(), calls=%async_computation.2 | async-start | bytes 2359296 | tf_op jit(solution)/shard_map/all_gather | solution.py:45
  402.1 519.0 %all-reduce.2.cloned.1.call-start = ((), (), s32[]{:S(2)}) async-start(), calls=%async_computation.3 | async-start | bytes 131072 | tf_op jit(solution)/shard_map/psum | solution.py:53
  812.0 110.6 %copy-start.1 = (s32[4,4]{1,0:T(4,128)S(1)}, s32[4,4]{1,0:T(4,128)}, u32[]{:S(2)}) copy-start(s32[4,4]{1,0:T(4,128)} %param.7) | copy-start | bytes 196
Sparse Core Ops, SparseCore 0:
  404.3 304.5 all-gather.1
  853.6 67.4 all-reduce.1
where the time goes:
time: 932 us; the launch traced here: 929 us
  waiting for transfers between devices  713 us (77%)
  local copies, waits for them, and re-layouts  107 us (11%)
  matrix products  78.7 us (8%)
  starting transfers between devices  16.5 us (2%)
  between operations  13.5 us (1%)
    all_to_all x1, waiting for transfers between devices, body(): lax.all_to_all(integrals, 'aux', split_axis=2, concat_axis=1, tiled=True)  317 us
    all_gather x1, waiting for transfers between devices, body(): lax.all_gather(metric, 'aux', axis=1, tiled=True)[0]  288 us
    psum x1, waiting for transfers between devices, body(): summed = lax.psum(partial_value, 'aux')  67.6 us
    dot_general x1, matrix products, body(): jnp.dot(lax.all_gather(metric, 'aux', axis=1, tiled=True)[0], columns, pr...  43.8 us
    all_to_all x1, waiting for transfers between devices, body(): lax.all_to_all(half_product[None], 'aux', split_axis=2, concat_axis=1, ti...  36 us
    squeeze x1, local copies, waits for them, and re-layouts, body(): half_moved[0]  25.3 us
    all_to_all x1, local copies, waits for them, and re-layouts, body(): lax.all_to_all(half_product[None], 'aux', split_axis=2, concat_axis=1, ti...  23.3 us
    unnamed x12, local copies, waits for them, and re-layouts  20.2 us
  transfers between devices with their start and end apart: 7, of which 6 were waited for; matrix products, arithmetic and copies ran while one was open for 11% of the time, Pallas kernels for 0%

commit v1 on v0

v1 whole, which is shorter than its diff:
```python
import functools

import jax
import jax.numpy as jnp
from jax import lax
from jax.experimental import pallas as pl
from jax.experimental.pallas import tpu as pltpu
from jax.sharding import PartitionSpec as P

RAD = 2
CHUNKS = 8
MESH = pl.DeviceIdType.MESH


def passed_along(block, axis, distance):
    devices = range(lax.axis_size(axis))
    route = [((i - distance) % len(devices), i) for i in devices]
    return lax.ppermute(block, axis, route)


def from_pair(block):
    return lax.ppermute(block, "dom", [(i ^ 1, i) for i in range(lax.axis_size("dom"))])


def move_kernel(n, i_ref, dt_ref, iout, hout, ibuf, held, stage,
                swap_send, swap_recv, i_send, i_recv, h_send, h_recv, loc, load):
    dom, aux = lax.axis_index("dom"), lax.axis_index("aux")
    half = n // 2
    core, side = dom % 2, aux // half
    base = dom - core
    partner = (base + 1 - core, (aux + half) % n)
    me = core * half + aux % half
    swaps = core != side
    block = jnp.where(swaps, (aux + half) % n, aux)
    rows, width = i_ref.shape[0], i_ref.shape[1]
    part, chunk = width // n, rows // CHUNKS

    def member(t):
        return (base + t // half, side * half + t % half)

    barrier = pltpu.get_barrier_semaphore()

    def greet(r, carry):
        pl.semaphore_signal(barrier, inc=1, device_id=member((me + r) % n), device_id_type=MESH)
        return carry

    lax.fori_loop(1, n, greet, 0)

    @pl.when(swaps)
    def _():
        pl.semaphore_signal(barrier, inc=1, device_id=partner, device_id_type=MESH)
        pl.semaphore_wait(barrier, n)

    @pl.when(jnp.logical_not(swaps))
    def _():
        pl.semaphore_wait(barrier, n - 1)

    def swap_copy(k):
        at = pl.ds(k * chunk, chunk)
        return pltpu.make_async_remote_copy(
            src_ref=i_ref.at[at], dst_ref=ibuf.at[at], send_sem=swap_send,
            recv_sem=swap_recv.at[k], device_id=partner, device_id_type=MESH)

    def spread(src, dst, at, send, recv):
        def one(r, carry):
            t = (me + r) % n
            pltpu.make_async_remote_copy(
                src_ref=src.at[at, pl.ds(pl.multiple_of(t * part, part), part)],
                dst_ref=dst.at[block, at],
                send_sem=send, recv_sem=recv,
                device_id=member(t), device_id_type=MESH).start()
            return carry
        lax.fori_loop(1, n, one, 0)

    def own(src, dst, at, sem):
        return pltpu.make_async_copy(
            src.at[at, pl.ds(pl.multiple_of(me * part, part), part)], dst.at[block, at], sem)

    def work(src, k):
        at = pl.ds(k * chunk, chunk)
        spread(src, iout, at, i_send, i_recv)
        own(src, iout, at, loc.at[0]).start()
        fetch = pltpu.make_async_copy(src.at[at], held, load)
        fetch.start()
        fetch.wait()

        def one(p, carry):
            stage[k * chunk + p] = jnp.dot(
                dt_ref[...], held[p], preferred_element_type=jnp.float32).astype(jnp.bfloat16)
            return carry
        lax.fori_loop(0, chunk, one, 0)
        spread(stage, hout, at, h_send, h_recv)
        own(stage, hout, at, loc.at[1]).start()

    @pl.when(swaps)
    def _():
        def begin(k, carry):
            swap_copy(k).start()
            return carry
        lax.fori_loop(0, CHUNKS, begin, 0)

        def step(k, carry):
            swap_copy(k).wait_recv()
            work(ibuf, k)
            return carry
        lax.fori_loop(0, CHUNKS, step, 0)
        pltpu.make_async_copy(i_ref, i_ref, swap_send).wait()

    @pl.when(jnp.logical_not(swaps))
    def _():
        def step(k, carry):
            work(i_ref, k)
            return carry
        lax.fori_loop(0, CHUNKS, step, 0)

    rest = pl.ds(0, n - 1)
    for out, s, r, l in ((iout, i_send, i_recv, 0), (hout, h_send, h_recv, 1)):
        pltpu.make_async_copy(out.at[0], out.at[0], loc.at[l]).wait()
        pltpu.make_async_copy(out.at[rest], out.at[rest], s).wait()
        pltpu.make_async_copy(out.at[rest], out.at[rest], r).wait()


def moved(ints, dt):
    n = lax.axis_size("aux")
    rows, width, cols = ints.shape
    shape = jax.ShapeDtypeStruct((n, rows, width // n, cols), ints.dtype)
    sem = pltpu.SemaphoreType.DMA
    return pl.pallas_call(
        functools.partial(move_kernel, n),
        out_shape=(shape, shape, jax.ShapeDtypeStruct(ints.shape, ints.dtype)),
        in_specs=[pl.BlockSpec(memory_space=pl.ANY), pl.BlockSpec(memory_space=pltpu.VMEM)],
        out_specs=[pl.BlockSpec(memory_space=pl.ANY)] * 3,
        scratch_shapes=[
            pltpu.VMEM((rows // CHUNKS, width, cols), ints.dtype),
            pltpu.VMEM((rows, width, cols), ints.dtype),
            sem, sem((CHUNKS,)), sem, sem, sem, sem, sem((2,)), sem,
        ],
        compiler_params=pltpu.CompilerParams(
            collective_id=0, has_side_effects=True, vmem_limit_bytes=40 * 2**20),
        cost_estimate=pl.CostEstimate(
            flops=2 * rows * width * width * cols, bytes_accessed=6 * rows * width * cols * 2,
            transcendentals=0),
    )(ints, dt)[:2]


def density_of(density, dens_cols, neighbours):
    domain_count = lax.axis_size("dom")
    my_domain = lax.axis_index("dom")
    size, count = density.shape[2], neighbours.shape[1]
    my_blocks = lax.dynamic_index_in_dim(neighbours, my_domain, 0, keepdims=False)
    slabs = jnp.stack([
        density[0] if offset == 0 else passed_along(density, "dom", -offset)[0]
        for offset in range(-RAD, RAD + 1)])
    slot = (my_blocks - my_domain + RAD) % domain_count
    listed = my_blocks[:, None] == jnp.arange(domain_count)[None]
    cols = jnp.sum(jnp.where(listed[:, :, None], dens_cols[None], 0), axis=1)
    matches = cols[:, None, :] == my_blocks[None, :, None]
    chosen = slot[:, None] == jnp.arange(2 * RAD + 1)[None]
    weight = (chosen[:, None, :, None] & matches[:, :, None, :]).astype(jnp.bfloat16)
    turned = jnp.einsum("jsok,okab->sbja", weight, slabs, preferred_element_type=jnp.float32)
    return turned.astype(jnp.bfloat16).reshape(count * size, count * size)


def body(integrals, density, dens_cols, neighbours, metric):
    n = lax.axis_size("aux")
    core, side = lax.axis_index("dom") % 2, lax.axis_index("aux") // (n // 2)
    stays = core == side
    mine = density_of(density, dens_cols, neighbours)
    dt = jnp.where(stays, mine, from_pair(mine))
    rows = lax.all_gather(metric[0], "aux", axis=0, tiled=True)
    rows = jnp.where(stays, rows, from_pair(rows))
    ints, half = moved(integrals[0], dt)
    ints = ints.reshape(-1, *ints.shape[2:])
    half = half.reshape(ints.shape)
    fitted = jnp.dot(
        rows, ints.reshape(ints.shape[0], -1), preferred_element_type=jnp.float32
    ).astype(jnp.bfloat16).reshape(ints.shape)
    part = jnp.einsum("psm,psn->mn", half, fitted, preferred_element_type=jnp.float32)
    spot = jnp.stack([jnp.where(side == 0, part, 0.0), jnp.where(side == 1, part, 0.0)])
    spot = lax.psum(spot, "aux")
    keep = jnp.where(core == 0, spot[0], spot[1])
    give = jnp.where(core == 0, spot[1], spot[0])
    return (keep + from_pair(give))[None]


def solution(mesh):
    return jax.shard_map(
        body,
        mesh=mesh,
        in_specs=(
            P("dom", "aux", None, None),
            P("dom", None, None, None),
            P(),
            P(),
            P("dom", "aux", None),
        ),
        out_specs=P("dom", None, None),
        check_vma=False,
    )
```

time: 932 us -> 766 us (0.82)
  waiting for transfers between devices: 713 us -> 127 us
  Pallas kernels: 0 us -> 536 us
  local copies, waits for them, and re-layouts: 107 us -> 18.9 us
  matrix products: 78.7 us -> 59.7 us
  starting transfers between devices: 16.5 us -> 5.46 us
    pallas_call x0 -> x1, Pallas kernels: none -> 536 us  [moved(): pl.pallas_call(functools.partial(move_kernel, n), out_shape=(shape, shape...]
    all_to_all x2 -> x0, waiting for transfers between devices: 353 us -> none  [the longest x1 317 us: body(): lax.all_to_all(integrals, 'aux', split_axis=2, concat_axis=1, tiled=True)]
    all_gather x1, waiting for transfers between devices: 288 us -> 46.8 us  [body(): rows = lax.all_gather(metric[0], 'aux', axis=0, tiled=True)]
    all_to_all x2 -> x0, local copies, waits for them, and re-layouts: 41.8 us -> none  [the longest x1 23.3 us: body(): lax.all_to_all(half_product[None], 'aux', split_axis=2, concat_axis=1, ti...]
    squeeze x1 -> x0, local copies, waits for them, and re-layouts: 25.3 us -> none  [body(): half_moved[0]]
    dot_general x4 -> x3, matrix products: 78.7 us -> 59.7 us  [the longest x1 44 us: body(): jnp.dot(rows, ints.reshape(ints.shape[0], -1), preferred_element_type=jnp...]
    broadcast_in_dim x1 -> x0, local copies, waits for them, and re-layouts: 18.6 us -> none  [body(): half_product[None]]
    all_to_all x2 -> x0, starting transfers between devices: 13.1 us -> none  [the longest x1 7.38 us: body(): lax.all_to_all(integrals, 'aux', split_axis=2, concat_axis=1, tiled=True)]
  transfers between devices with their start and end apart: 7 -> 8, of which waited for: 6 -> 4; matrix products, arithmetic and copies ran while one was open for 11% -> 1% of each run, Pallas kernels for 0% -> 70%
where the time goes in v1:
time: 766 us; the launch traced here: 765 us
  Pallas kernels  536 us (70%)
  waiting for transfers between devices  127 us (17%)
  matrix products  59.7 us (8%)
  local copies, waits for them, and re-layouts  18.9 us (2%)
  between operations  13.5 us (2%)
    pallas_call x1, Pallas kernels, moved(): pl.pallas_call(functools.partial(move_kernel, n), out_shape=(shape, shape...  536 us
    psum x1, waiting for transfers between devices, body(): spot = lax.psum(spot, 'aux')  76.5 us
    all_gather x1, waiting for transfers between devices, body(): rows = lax.all_gather(metric[0], 'aux', axis=0, tiled=True)  46.8 us
    dot_general x1, matrix products, body(): jnp.dot(rows, ints.reshape(ints.shape[0], -1), preferred_element_type=jnp...  44 us
    unnamed x5, local copies, waits for them, and re-layouts  16.3 us
  transfers between devices with their start and end apart: 8, of which 4 were waited for; matrix products, arithmetic and copies ran while one was open for 1% of the time, Pallas kernels for 70%

profile of v1, /device:TPU:0, one launch (start us, length us, event | category | flops | bytes accessed | tf_op | source)
XLA Modules:
  0.0 765.3 jit_solution(2897305706968113469)
XLA Ops:
  6.5 0.0 all-gather.3.cloned.1.call-start
  6.5 0.7 all-gather.3.cloned.1.call-update
  7.3 0.0 all-reduce.2.cloned.1.call-start
  7.3 1.1 copy.13
  8.4 3.0 collective-permute-start
  11.4 0.0 collective-permute-start.1
  11.4 1.7 collective-permute-start.2
  13.2 0.7 and_select_fusion
  13.9 0.1 iota_compare_fusion
  14.0 0.8 select_reduce_fusion
  14.7 46.8 %all-gather.3.cloned.1.call-done = bf16[1,1024,1024]{2,1,0:T(8,128)(2,1)} async-done(((bf16[1,128,1024]{2,1,0:T(8,128)(2,1)}), bf16[1,1024,1024]{2,1,0:T(8,128)(2,1)}) %all-gather.3.cloned.1.call-update) | async-done | bytes 2097168 | tf_op jit(solution)/shard_map/all_gather | solution.py:170
  61.5 0.0 collective-permute-start.4
  61.5 0.1 broadcast_compare_fusion
  61.6 0.1 iota_compare_fusion.1
  61.7 0.0 collective-permute-done
  61.7 0.0 collective-permute-done.1
  61.7 0.0 collective-permute-done.2
  61.7 2.1 stack.12
  63.8 0.6 fusion.8
  64.4 0.5 copy.17
  64.9 0.1 copy.36
  65.0 0.6 collective-permute-start.3
  65.6 1.5 collective-permute-done.3
  67.1 0.1 broadcast_select_fusion.dt_ref
  67.2 0.0 copy-start
  67.2 536.1 %shard_map.55 = (bf16[8,128,64,128]{3,2,1,0:T(8,128)(2,1)}, bf16[8,128,64,128]{3,2,1,0:T(8,128)(2,1)}, bf16[128,512,128]{2,1,0:T(8,128)(2,1)}) custom-call(bf16[128,512,128]{2,1,0:T(8,128)(2,1)} %bitcast.66, bf16[512,512]{1,0:T(8,128)(2,1)S(1)} %broadcast_select_fusion.dt_ref), custom_call_target="tpu_custom_call" | custom-call | flops 8589934592 | bytes 100663296 | tf_op jit(solution)/shard_map/pallas_call | solution.py:128
  603.3 0.0 collective-permute-done.4
  603.3 0.0 copy-done
  603.3 44.0 %convert_bitcast_fusion = bf16[128,8,64,128]{3,1,2,0:T(8,128)(2,1)} fusion(bf16[128,8,64,128]{3,2,1,0:T(8,128)(2,1)} %bitcast.69, bf16[1024,1024]{1,0:T(8,128)(2,1)} %collective-permute-done.4, pred[]{:T(512)S(6)} %eq.70, bf16[1,1024,1024]{2,1,0:T(8,128)(2,1)S(1)} %copy-done), kind=kOutput, calls=%fused_computation.3 | convolution fusion | flops 17189306368 | bytes 37748736 | tf_op jit(solution)/shard_map/dot_general | solution.py:175
  647.3 15.1 %copy.26 = bf16[128,8,64,128]{3,2,1,0:T(8,128)(2,1)} copy(bf16[128,8,64,128]{3,1,2,0:T(8,128)(2,1)} %convert_bitcast_fusion) | data formatting | bytes 33554432
  662.3 15.1 %select_bitcast_fusion.2 = (f32[1,128,128]{2,1,0:T(8,128)S(1)}, f32[1,128,128]{2,1,0:T(8,128)S(1)}) fusion(pred[]{:T(512)S(6)} %eq.69, pred[]{:T(512)S(6)} %eq.80, bf16[1024,64,128]{2,1,0:T(8,128)(2,1)} %bitcast.68, bf16[1024,64,128]{2,1,0:T(8,128)(2,1)} %bitcast.62), kind=kOutput, calls=%fused_computation.18 | convolution fusion | flops 2147516416 | bytes 33685504 | tf_op jit(solution)/shard_map/psm,psn->mn/dot_general | solution.py:178
  677.5 0.7 pad_maximum_fusion
  678.1 0.0 all-reduce.2.cloned.1.call-update
  678.2 76.5 %all-reduce.2.cloned.1.call-done = f32[2,128,128]{2,1,0:T(8,128)} async-done(((f32[2,128,128]{2,1,0:T(8,128)}), f32[2,128,128]{2,1,0:T(8,128)}) %all-reduce.2.cloned.1.call-update) | async-done | bytes 131088 | tf_op jit(solution)/shard_map/psum | solution.py:180
  754.7 0.9 select_bitcast_fusion
  755.6 0.1 collective-permute-start.5
  755.7 1.2 collective-permute-done.5
  756.9 1.5 fusion.10
Async XLA Ops:
  6.5 55.0 %all-gather.3.cloned.1.call-start = ((), (), s32[]{:S(2)}) async-start(), calls=%async_computation.1 | async-start | bytes 2359296 | tf_op jit(solution)/shard_map/all_gather | solution.py:170
  7.3 747.5 %all-reduce.2.cloned.1.call-start = ((), (), s32[]{:S(2)}) async-start(), calls=%async_computation | async-start | bytes 262144 | tf_op jit(solution)/shard_map/psum | solution.py:180
  8.4 53.2 %collective-permute-start = (bf16[1,4,128,128]{3,0,1,2:T(2,128)(2,1)S(1)}, bf16[1,4,128,128]{3,0,1,2:T(2,128)(2,1)S(1)}, u32[]{:S(2)}, u32[]{:S(2)}) collective-permute-start(bf16[1,4,128,128]{3,0,1,2:T(2,128)(2,1)S(1)} %copy.13), channel_id=1, source_target_pairs={{16,0},{24,8},{0,16},{8,24},{17,1},{25,9},{1,17},{9,25},{18,2},{26... | collective-permute-start | bytes 393224 | tf_op jit(solution)/shard_map/ppermute | solution.py:18
  11.4 50.2 %collective-permute-start.1 = (bf16[1,4,128,128]{3,0,1,2:T(2,128)(2,1)S(1)}, bf16[1,4,128,128]{3,0,1,2:T(2,128)(2,1)S(1)}, u32[]{:S(2)}, u32[]{:S(2)}) collective-permute-start(bf16[1,4,128,128]{3,0,1,2:T(2,128)(2,1)S(1)} %copy.13), channel_id=1, source_target_pairs={{24,0},{0,8},{8,16},{16,24},{25,1},{1,9},{9,17},{17,25},{26,2},{2,... | collective-permute-start | bytes 393224 | tf_op jit(solution)/shard_map/ppermute | solution.py:18
  11.4 50.2 %collective-permute-start.2 = (bf16[1,4,128,128]{3,0,1,2:T(2,128)(2,1)S(1)}, bf16[1,4,128,128]{3,0,1,2:T(2,128)(2,1)S(1)}, u32[]{:S(2)}, u32[]{:S(2)}) collective-permute-start(bf16[1,4,128,128]{3,0,1,2:T(2,128)(2,1)S(1)} %copy.13), channel_id=1, source_target_pairs={{8,0},{16,8},{24,16},{0,24},{9,1},{17,9},{25,17},{1,25},{10,2},{18... | collective-permute-start | bytes 393224 | tf_op jit(solution)/shard_map/ppermute | solution.py:18
  61.5 541.8 %collective-permute-start.4 = (bf16[1024,1024]{1,0:T(8,128)(2,1)}, bf16[1024,1024]{1,0:T(8,128)(2,1)}, u32[]{:S(2)}, u32[]{:S(2)}) collective-permute-start(bf16[1024,1024]{1,0:T(8,128)(2,1)} %bitcast.67), channel_id=1, source_target_pairs={{8,0},{0,8},{24,16},{16,24},{9,1},{1,9},{25,17},{17,25},{10,2},{2,... | collective-permute-start | bytes 6291464 | tf_op jit(solution)/shard_map/ppermute | solution.py:22
  65.0 2.1 collective-permute-start.3
  67.2 536.1 %copy-start = (bf16[1,1024,1024]{2,1,0:T(8,128)(2,1)S(1)}, bf16[1,1024,1024]{2,1,0:T(8,128)(2,1)}, u32[]{:S(2)}) copy-start(bf16[1,1024,1024]{2,1,0:T(8,128)(2,1)} %all-gather.3.cloned.1.call-done) | copy-start | bytes 6291460
  755.6 1.3 collective-permute-start.5
Sparse Core Ops, SparseCore 0:
  9.5 51.9 all-gather.2
  678.3 76.3 all-reduce.1

commit v2 on v1

--- a/solution.py
+++ b/solution.py
@@ -22,8 +22,7 @@
     return lax.ppermute(block, "dom", [(i ^ 1, i) for i in range(lax.axis_size("dom"))])
 
 
-def move_kernel(n, i_ref, dt_ref, iout, hout, ibuf, held, stage,
-                swap_send, swap_recv, i_send, i_recv, h_send, h_recv, loc, load):
+def place(n):
     dom, aux = lax.axis_index("dom"), lax.axis_index("aux")
     half = n // 2
     core, side = dom % 2, aux // half
@@ -32,12 +31,14 @@
     me = core * half + aux % half
     swaps = core != side
     block = jnp.where(swaps, (aux + half) % n, aux)
-    rows, width = i_ref.shape[0], i_ref.shape[1]
-    part, chunk = width // n, rows // CHUNKS
 
     def member(t):
         return (base + t // half, side * half + t % half)
 
+    return partner, me, swaps, block, member
+
+
+def meet(n, partner, me, swaps, member):
     barrier = pltpu.get_barrier_semaphore()
 
     def greet(r, carry):
@@ -54,6 +55,34 @@
     @pl.when(jnp.logical_not(swaps))
     def _():
         pl.semaphore_wait(barrier, n - 1)
+
+
+def move_kernel(n, i_ref, dt_ref, m_ref, iout, hout, mout, ibuf, mbuf, held, stage,
+                swap_send, swap_recv, i_send, i_recv, h_send, h_recv, loc, load,
+                m_swap, m_send, m_recv, m_pair, m_loc):
+    half = n // 2
+    partner, me, swaps, block, member = place(n)
+    rows, width = i_ref.shape[0], i_ref.shape[1]
+    part, chunk = width // n, rows // CHUNKS
+    meet(n, partner, me, swaps, member)
+    other = member((me + half) % n)
+    first = block // half * half
+
+    def swap_metric():
+        return pltpu.make_async_remote_copy(
+            src_ref=m_ref, dst_ref=mbuf, send_sem=m_swap.at[0], recv_sem=m_swap.at[1],
+            device_id=partner, device_id_type=MESH)
+
+    def spread_metric(src):
+        pltpu.make_async_copy(src, mout.at[block], m_loc).start()
+
+        def one(r, carry):
+            t = me // half * half + (me + r) % half
+            pltpu.make_async_remote_copy(
+                src_ref=src, dst_ref=mout.at[block], send_sem=m_send, recv_sem=m_recv,
+                device_id=member(t), device_id_type=MESH).start()
+            return carry
+        lax.fori_loop(1, half, one, 0)
 
     def swap_copy(k):
         at = pl.ds(k * chunk, chunk)
@@ -94,10 +123,14 @@
 
     @pl.when(swaps)
     def _():
+        swap_metric().start()
+
         def begin(k, carry):
             swap_copy(k).start()
             return carry
         lax.fori_loop(0, CHUNKS, begin, 0)
+        swap_metric().wait()
+        spread_metric(mbuf)
 
         def step(k, carry):
             swap_copy(k).wait_recv()
@@ -108,10 +141,23 @@
 
     @pl.when(jnp.logical_not(swaps))
     def _():
+        spread_metric(m_ref)
+
         def step(k, carry):
             work(i_ref, k)
             return carry
         lax.fori_loop(0, CHUNKS, step, 0)
+
+    pltpu.make_async_copy(m_ref, mout.at[block], m_loc).wait()
+    few = mout.at[pl.ds(0, half - 1)]
+    pltpu.make_async_copy(few, few, m_send).wait()
+    pltpu.make_async_copy(few, few, m_recv).wait()
+    lot = mout.at[pl.ds(first, half)]
+    share = pltpu.make_async_remote_copy(
+        src_ref=lot, dst_ref=lot, send_sem=m_pair.at[0], recv_sem=m_pair.at[1],
+        device_id=other, device_id_type=MESH)
+    share.start()
+    share.wait()
 
     rest = pl.ds(0, n - 1)
     for out, s, r, l in ((iout, i_send, i_recv, 0), (hout, h_send, h_recv, 1)):
@@ -120,27 +166,83 @@
         pltpu.make_async_copy(out.at[rest], out.at[rest], r).wait()
 
 
-def moved(ints, dt):
+def sum_kernel(n, e_ref, out_ref, parts, total, swap, send, recv):
+    partner, me, swaps, block, member = place(n)
+    meet(n, partner, me, swaps, member)
+
+    def one(r, carry):
+        pltpu.make_async_remote_copy(
+            src_ref=e_ref, dst_ref=parts.at[me], send_sem=send, recv_sem=recv,
+            device_id=member((me + r) % n), device_id_type=MESH).start()
+        return carry
+    lax.fori_loop(1, n, one, 0)
+    parts[me] = e_ref[...]
+    rest = parts.at[pl.ds(0, n - 1)]
+    pltpu.make_async_copy(rest, rest, recv).wait()
+    pltpu.make_async_copy(rest, rest, send).wait()
+    total[...] = parts[0]
+
+    def add(t, carry):
+        total[...] += parts[t]
+        return carry
+    lax.fori_loop(1, n, add, 0)
+
+    @pl.when(swaps)
+    def _():
+        copy = pltpu.make_async_remote_copy(
+            src_ref=total, dst_ref=out_ref, send_sem=swap.at[0], recv_sem=swap.at[1],
+            device_id=partner, device_id_type=MESH)
+        copy.start()
+        copy.wait()
+
+    @pl.when(jnp.logical_not(swaps))
+    def _():
+        out_ref[...] = total[...]
+
+
+def summed(part):
+    n = lax.axis_size("aux")
+    sem = pltpu.SemaphoreType.DMA
+    vmem = pl.BlockSpec(memory_space=pltpu.VMEM)
+    return pl.pallas_call(
+        functools.partial(sum_kernel, n),
+        out_shape=jax.ShapeDtypeStruct(part.shape, part.dtype),
+        in_specs=[vmem],
+        out_specs=vmem,
+        scratch_shapes=[
+            pltpu.VMEM((n, *part.shape), part.dtype), pltpu.VMEM(part.shape, part.dtype),
+            sem((2,)), sem, sem],
+        compiler_params=pltpu.CompilerParams(collective_id=1, has_side_effects=True),
+    )(part)
+
+
+def moved(ints, dt, metric):
     n = lax.axis_size("aux")
     rows, width, cols = ints.shape
     shape = jax.ShapeDtypeStruct((n, rows, width // n, cols), ints.dtype)
     sem = pltpu.SemaphoreType.DMA
     return pl.pallas_call(
         functools.partial(move_kernel, n),
-        out_shape=(shape, shape, jax.ShapeDtypeStruct(ints.shape, ints.dtype)),
-        in_specs=[pl.BlockSpec(memory_space=pl.ANY), pl.BlockSpec(memory_space=pltpu.VMEM)],
-        out_specs=[pl.BlockSpec(memory_space=pl.ANY)] * 3,
+        out_shape=(
+            shape, shape, jax.ShapeDtypeStruct((n, *metric.shape), metric.dtype),
+            jax.ShapeDtypeStruct(ints.shape, ints.dtype),
+            jax.ShapeDtypeStruct(metric.shape, metric.dtype)),
+        in_specs=[
+            pl.BlockSpec(memory_space=pl.ANY), pl.BlockSpec(memory_space=pltpu.VMEM),
+            pl.BlockSpec(memory_space=pl.ANY)],
+        out_specs=[pl.BlockSpec(memory_space=pl.ANY)] * 5,
         scratch_shapes=[
             pltpu.VMEM((rows // CHUNKS, width, cols), ints.dtype),
             pltpu.VMEM((rows, width, cols), ints.dtype),
             sem, sem((CHUNKS,)), sem, sem, sem, sem, sem((2,)), sem,
+            sem((2,)), sem, sem, sem((2,)), sem,
         ],
         compiler_params=pltpu.CompilerParams(
             collective_id=0, has_side_effects=True, vmem_limit_bytes=40 * 2**20),
         cost_estimate=pl.CostEstimate(
             flops=2 * rows * width * width * cols, bytes_accessed=6 * rows * width * cols * 2,
             transcendentals=0),
-    )(ints, dt)[:2]
+    )(ints, dt, metric)[:3]
 
 
 def density_of(density, dens_cols, neighbours):
@@ -167,20 +269,15 @@
     stays = core == side
     mine = density_of(density, dens_cols, neighbours)
     dt = jnp.where(stays, mine, from_pair(mine))
-    rows = lax.all_gather(metric[0], "aux", axis=0, tiled=True)
-    rows = jnp.where(stays, rows, from_pair(rows))
-    ints, half = moved(integrals[0], dt)
+    ints, half, rows = moved(integrals[0], dt, metric[0])
+    rows = rows.reshape(-1, rows.shape[2])
     ints = ints.reshape(-1, *ints.shape[2:])
     half = half.reshape(ints.shape)
     fitted = jnp.dot(
         rows, ints.reshape(ints.shape[0], -1), preferred_element_type=jnp.float32
     ).astype(jnp.bfloat16).reshape(ints.shape)
     part = jnp.einsum("psm,psn->mn", half, fitted, preferred_element_type=jnp.float32)
-    spot = jnp.stack([jnp.where(side == 0, part, 0.0), jnp.where(side == 1, part, 0.0)])
-    spot = lax.psum(spot, "aux")
-    keep = jnp.where(core == 0, spot[0], spot[1])
-    give = jnp.where(core == 0, spot[1], spot[0])
-    return (keep + from_pair(give))[None]
+    return summed(part)[None]
 
 
 def solution(mesh):

time: 766 us -> 682 us (0.89)
  waiting for transfers between devices: 127 us -> 11.2 us
  Pallas kernels: 536 us -> 569 us
  between operations: 13.5 us -> 0.07 us
  matrix products: 59.7 us -> 69.1 us
    psum x1 -> x0, waiting for transfers between devices: 76.5 us -> none  [body(): spot = lax.psum(spot, 'aux')]
    all_gather x1 -> x0, waiting for transfers between devices: 46.8 us -> none  [body(): rows = lax.all_gather(metric[0], 'aux', axis=0, tiled=True)]
    pallas_call x0 -> x1, Pallas kernels: none -> 18.8 us  [summed(): pl.pallas_call(functools.partial(sum_kernel, n), out_shape=jax.ShapeDtype...]
    pallas_call x1, Pallas kernels: 536 us -> 550 us  [moved(): pl.pallas_call(functools.partial(move_kernel, n), out_shape=(shape, shape...]
    ppermute x3, waiting for transfers between devices: 0.01 us -> 9.71 us  [passed_along(): return lax.ppermute(block, axis, route)]
    dot_general x1, matrix products: 44 us -> 52.7 us  [body(): jnp.dot(rows, ints.reshape(ints.shape[0], -1), preferred_element_type=jnp...]
    unnamed x5 -> x6, local copies, waits for them, and re-layouts: 16.3 us -> 18.7 us
  transfers between devices with their start and end apart: 8 -> 4, of which waited for: 4 -> 4; matrix products, arithmetic and copies ran while one was open for 1% -> 0% of each run, Pallas kernels for 70% -> 0%
where the time goes in v2:
time: 682 us; the launch traced here: 677 us
  Pallas kernels  569 us (83%)
  matrix products  69.1 us (10%)
  local copies, waits for them, and re-layouts  21.3 us (3%)
  waiting for transfers between devices  11.2 us (2%)
    pallas_call x1, Pallas kernels, moved(): pl.pallas_call(functools.partial(move_kernel, n), out_shape=(shape, shape...  550 us
    dot_general x1, matrix products, body(): jnp.dot(rows, ints.reshape(ints.shape[0], -1), preferred_element_type=jnp...  52.7 us
    pallas_call x1, Pallas kernels, summed(): pl.pallas_call(functools.partial(sum_kernel, n), out_shape=jax.ShapeDtype...  18.8 us
    unnamed x6, local copies, waits for them, and re-layouts  18.7 us
    dot_general x1, matrix products, body(): jnp.einsum('psm,psn->mn', half, fitted, preferred_element_type=jnp.float32)  15.7 us
  transfers between devices with their start and end apart: 4, of which 4 were waited for; matrix products, arithmetic and copies ran while one was open for 0% of the time, Pallas kernels for 0%

profile of v2, /device:TPU:0, one launch (start us, length us, event | category | flops | bytes accessed | tf_op | source)
XLA Modules:
  0.0 676.6 jit_solution(338711388043894410)
XLA Ops:
  0.0 1.1 copy.13
  1.1 2.5 collective-permute-start.2
  3.6 0.0 collective-permute-start.1
  3.6 1.1 collective-permute-start
  4.6 0.7 and_select_fusion
  5.3 0.1 iota_compare_fusion
  5.4 0.8 select_reduce_fusion
  6.2 0.1 broadcast_compare_fusion
  6.3 0.1 iota_compare_fusion.1
  6.3 3.9 collective-permute-done.2
  10.2 1.9 collective-permute-done.1
  12.2 3.9 collective-permute-done
  16.0 2.1 stack.3
  18.1 0.6 fusion.6
  18.7 0.5 copy.17
  19.3 0.1 copy.36
  19.4 0.8 collective-permute-start.3
  20.1 1.5 collective-permute-done.3
  21.7 0.1 broadcast_select_fusion.dt_ref
  21.8 0.0 copy-start
  21.8 0.9 copy-done
  22.7 550.0 %shard_map.55 = (bf16[8,128,64,128]{3,2,1,0:T(8,128)(2,1)}, bf16[8,128,64,128]{3,2,1,0:T(8,128)(2,1)}, bf16[8,128,1024]{2,1,0:T(8,128)(2,1)S(1)}, bf16[128,512,128]{2,1,0:T(8,128)(2,1)}, bf16[128,1024]{1,0:T(8,128)(2,1)}) custom-call(bf16[128,512,128]{2,1,0:T(8,128)(2,1)} %bitcast.54, bf16[512,512]{1,0:T(8,128)(2,1)S(1)} %broadcast_select_fusion.dt_ref, ...), custom_call_target="tpu_custom_call" | custom-call | flops 8589934592 | bytes 100663296 | tf_op jit(solution)/shard_map/pallas_call | solution.py:224
  572.7 52.7 %convert_bitcast_fusion = bf16[128,8,64,128]{3,1,2,0:T(8,128)(2,1)} fusion(bf16[1024,1024]{1,0:T(8,128)(2,1)S(1)} %bitcast.48, bf16[128,8,64,128]{3,2,1,0:T(8,128)(2,1)} %bitcast.56), kind=kOutput, calls=%fused_computation.3 | convolution fusion | flops 17188257792 | bytes 35651584 | tf_op jit(solution)/shard_map/dot_general | solution.py:276
  625.5 15.1 %copy.26 = bf16[128,8,64,128]{3,2,1,0:T(8,128)(2,1)} copy(bf16[128,8,64,128]{3,1,2,0:T(8,128)(2,1)} %convert_bitcast_fusion) | data formatting | bytes 33554432
  640.6 15.7 %convolution_bitcast_fusion.1.e_ref = f32[128,128]{1,0:T(8,128)} fusion(bf16[1024,64,128]{2,1,0:T(8,128)(2,1)} %bitcast.55, bf16[1024,64,128]{2,1,0:T(8,128)(2,1)} %bitcast.49), kind=kOutput, calls=%fused_computation.7 | convolution fusion | flops 2147483648 | bytes 33619968 | tf_op jit(solution)/shard_map/psm,psn->mn/dot_general | solution.py:279
  656.3 18.8 %shard_map.56 = f32[128,128]{1,0:T(8,128)} custom-call(f32[128,128]{1,0:T(8,128)} %convolution_bitcast_fusion.1.e_ref), custom_call_target="tpu_custom_call" | custom-call | tf_op jit(solution)/shard_map/pallas_call | solution.py:207
  675.1 1.5 copy.38
Async XLA Ops:
  1.1 9.1 %collective-permute-start.2 = (bf16[1,4,128,128]{3,0,1,2:T(2,128)(2,1)S(1)}, bf16[1,4,128,128]{3,0,1,2:T(2,128)(2,1)S(1)}, u32[]{:S(2)}, u32[]{:S(2)}) collective-permute-start(bf16[1,4,128,128]{3,0,1,2:T(2,128)(2,1)S(1)} %copy.13), channel_id=1, source_target_pairs={{8,0},{16,8},{24,16},{0,24},{9,1},{17,9},{25,17},{1,25},{10,2},{18... | collective-permute-start | bytes 393224 | tf_op jit(solution)/shard_map/ppermute | solution.py:18
  3.6 8.6 %collective-permute-start.1 = (bf16[1,4,128,128]{3,0,1,2:T(2,128)(2,1)S(1)}, bf16[1,4,128,128]{3,0,1,2:T(2,128)(2,1)S(1)}, u32[]{:S(2)}, u32[]{:S(2)}) collective-permute-start(bf16[1,4,128,128]{3,0,1,2:T(2,128)(2,1)S(1)} %copy.13), channel_id=1, source_target_pairs={{24,0},{0,8},{8,16},{16,24},{25,1},{1,9},{9,17},{17,25},{26,2},{2,... | collective-permute-start | bytes 393224 | tf_op jit(solution)/shard_map/ppermute | solution.py:18
  3.6 12.5 %collective-permute-start = (bf16[1,4,128,128]{3,0,1,2:T(2,128)(2,1)S(1)}, bf16[1,4,128,128]{3,0,1,2:T(2,128)(2,1)S(1)}, u32[]{:S(2)}, u32[]{:S(2)}) collective-permute-start(bf16[1,4,128,128]{3,0,1,2:T(2,128)(2,1)S(1)} %copy.13), channel_id=1, source_target_pairs={{16,0},{24,8},{0,16},{8,24},{17,1},{25,9},{1,17},{9,25},{18,2},{26... | collective-permute-start | bytes 393224 | tf_op jit(solution)/shard_map/ppermute | solution.py:18
  19.4 2.3 collective-permute-start.3
  21.8 1.0 copy-start

commit v3 on v2

--- a/solution.py
+++ b/solution.py
@@ -245,6 +245,40 @@
     )(ints, dt, metric)[:3]
 
 
+def share_kernel(m_ref, i_ref, h_ref, e_ref):
+    @pl.when(pl.program_id(0) == 0)
+    def _():
+        e_ref[...] = jnp.zeros_like(e_ref)
+
+    ints = jnp.swapaxes(i_ref[...], 0, 1)
+    half = jnp.swapaxes(h_ref[...], 0, 1)
+    cols = ints.shape[2]
+    total = jnp.zeros(e_ref.shape, jnp.float32)
+    for s in range(0, ints.shape[0], 2):
+        pair = jnp.concatenate([ints[s], ints[s + 1]], axis=1)
+        fitted = jnp.dot(
+            m_ref[...], pair, preferred_element_type=jnp.float32).astype(jnp.bfloat16)
+        for o in range(2):
+            total += lax.dot_general(
+                half[s + o], fitted[:, o * cols:(o + 1) * cols], (((0,), (0,)), ((), ())),
+                preferred_element_type=jnp.float32)
+    e_ref[...] += total
+
+
+def share_of(rows, ints, half):
+    count, width, cols = ints.shape
+    step = min(16, width)
+    block = pl.BlockSpec((count, step, cols), lambda s: (0, s, 0))
+    return pl.pallas_call(
+        share_kernel,
+        grid=(width // step,),
+        out_shape=jax.ShapeDtypeStruct((cols, cols), jnp.float32),
+        in_specs=[pl.BlockSpec(memory_space=pltpu.VMEM), block, block],
+        out_specs=pl.BlockSpec((cols, cols), lambda s: (0, 0)),
+        compiler_params=pltpu.CompilerParams(vmem_limit_bytes=56 * 2**20),
+    )(rows, ints, half)
+
+
 def density_of(density, dens_cols, neighbours):
     domain_count = lax.axis_size("dom")
     my_domain = lax.axis_index("dom")
@@ -271,12 +305,7 @@
     dt = jnp.where(stays, mine, from_pair(mine))
     ints, half, rows = moved(integrals[0], dt, metric[0])
     rows = rows.reshape(-1, rows.shape[2])
-    ints = ints.reshape(-1, *ints.shape[2:])
-    half = half.reshape(ints.shape)
-    fitted = jnp.dot(
-        rows, ints.reshape(ints.shape[0], -1), preferred_element_type=jnp.float32
-    ).astype(jnp.bfloat16).reshape(ints.shape)
-    part = jnp.einsum("psm,psn->mn", half, fitted, preferred_element_type=jnp.float32)
+    part = share_of(rows, ints.reshape(-1, *ints.shape[2:]), half.reshape(-1, *half.shape[2:]))
     return summed(part)[None]
 
 

time: 682 us -> 648 us (0.950)
  matrix products: 69.1 us -> 0.59 us
  Pallas kernels: 569 us -> 618 us
  local copies, waits for them, and re-layouts: 21.3 us -> 7.57 us
    dot_general x2 -> x0, matrix products: 68.5 us -> none  [the longest x1 52.7 us: body(): jnp.dot(rows, ints.reshape(ints.shape[0], -1), preferred_element_type=jnp...]
    pallas_call x0 -> x1, Pallas kernels: none -> 48.9 us  [share_of(): pl.pallas_call(share_kernel, grid=(width // step,), out_shape=jax.ShapeDt...]
    unnamed x6 -> x7, local copies, waits for them, and re-layouts: 18.7 us -> 4.93 us
where the time goes in v3:
time: 648 us; the launch traced here: 643 us
  Pallas kernels  618 us (95%)
  waiting for transfers between devices  11.2 us (2%)
  local copies, waits for them, and re-layouts  7.57 us (1%)
    pallas_call x1, Pallas kernels, moved(): pl.pallas_call(functools.partial(move_kernel, n), out_shape=(shape, shape...  550 us
    pallas_call x1, Pallas kernels, share_of(): pl.pallas_call(share_kernel, grid=(width // step,), out_shape=jax.ShapeDt...  48.9 us
    pallas_call x1, Pallas kernels, summed(): pl.pallas_call(functools.partial(sum_kernel, n), out_shape=jax.ShapeDtype...  18.7 us
  transfers between devices with their start and end apart: 4, of which 4 were waited for; matrix products, arithmetic and copies ran while one was open for 0% of the time, Pallas kernels for 0%

profile of v3, /device:TPU:0, one launch (start us, length us, event | category | flops | bytes accessed | tf_op | source)
XLA Modules:
  0.0 643.2 jit_solution(12526629626582308813)
XLA Ops:
  0.0 1.1 copy.11
  1.1 2.5 collective-permute-start.2
  3.6 0.0 collective-permute-start.1
  3.6 1.1 collective-permute-start
  4.6 0.7 and_select_fusion
  5.3 0.1 iota_compare_fusion
  5.4 0.8 select_reduce_fusion
  6.2 0.1 broadcast_compare_fusion
  6.3 0.1 iota_compare_fusion.1
  6.3 3.9 collective-permute-done.2
  10.2 1.9 collective-permute-done.1
  12.2 3.9 collective-permute-done
  16.0 2.1 stack.3
  18.1 0.6 fusion.1
  18.7 0.5 copy.15
  19.3 0.1 copy.22
  19.4 0.8 collective-permute-start.3
  20.1 1.5 collective-permute-done.3
  21.7 0.1 broadcast_select_fusion.dt_ref
  21.7 0.0 copy-start.1
  21.8 0.9 copy-done.1
  22.7 550.0 %shard_map.55 = (bf16[8,128,64,128]{3,2,1,0:T(8,128)(2,1)}, bf16[8,128,64,128]{3,2,1,0:T(8,128)(2,1)}, bf16[8,128,1024]{2,1,0:T(8,128)(2,1)S(1)}, bf16[128,512,128]{2,1,0:T(8,128)(2,1)}, bf16[128,1024]{1,0:T(8,128)(2,1)}) custom-call(bf16[128,512,128]{2,1,0:T(8,128)(2,1)} %bitcast.41, bf16[512,512]{1,0:T(8,128)(2,1)S(1)} %broadcast_select_fusion.dt_ref, ...), custom_call_target="tpu_custom_call" | custom-call | flops 8589934592 | bytes 100663296 | tf_op jit(solution)/shard_map/pallas_call | solution.py:224
  572.7 0.0 copy-start
  572.7 1.3 copy-done
  574.1 48.9 %shard_map.56.e_ref = f32[128,128]{1,0:T(8,128)} custom-call(bf16[1024,1024]{1,0:T(8,128)(2,1)} %bitcast.33, bf16[1024,64,128]{2,1,0:T(8,128)(2,1)} %bitcast.35, bf16[1024,64,128]{2,1,0:T(8,128)(2,1)} %bitcast.36), custom_call_target="tpu_custom_call" | custom-call | tf_op jit(solution)/shard_map/pallas_call | solution.py:272
  623.0 18.7 %shard_map.57 = f32[128,128]{1,0:T(8,128)} custom-call(f32[128,128]{1,0:T(8,128)} %shard_map.56.e_ref), custom_call_target="tpu_custom_call" | custom-call | tf_op jit(solution)/shard_map/pallas_call | solution.py:207
  641.7 1.5 copy.24
Async XLA Ops:
  1.1 9.1 %collective-permute-start.2 = (bf16[1,4,128,128]{3,0,1,2:T(2,128)(2,1)S(1)}, bf16[1,4,128,128]{3,0,1,2:T(2,128)(2,1)S(1)}, u32[]{:S(2)}, u32[]{:S(2)}) collective-permute-start(bf16[1,4,128,128]{3,0,1,2:T(2,128)(2,1)S(1)} %copy.11), channel_id=1, source_target_pairs={{8,0},{16,8},{24,16},{0,24},{9,1},{17,9},{25,17},{1,25},{10,2},{18... | collective-permute-start | bytes 393224 | tf_op jit(solution)/shard_map/ppermute | solution.py:18
  3.6 8.6 %collective-permute-start.1 = (bf16[1,4,128,128]{3,0,1,2:T(2,128)(2,1)S(1)}, bf16[1,4,128,128]{3,0,1,2:T(2,128)(2,1)S(1)}, u32[]{:S(2)}, u32[]{:S(2)}) collective-permute-start(bf16[1,4,128,128]{3,0,1,2:T(2,128)(2,1)S(1)} %copy.11), channel_id=1, source_target_pairs={{24,0},{0,8},{8,16},{16,24},{25,1},{1,9},{9,17},{17,25},{26,2},{2,... | collective-permute-start | bytes 393224 | tf_op jit(solution)/shard_map/ppermute | solution.py:18
  3.6 12.5 %collective-permute-start = (bf16[1,4,128,128]{3,0,1,2:T(2,128)(2,1)S(1)}, bf16[1,4,128,128]{3,0,1,2:T(2,128)(2,1)S(1)}, u32[]{:S(2)}, u32[]{:S(2)}) collective-permute-start(bf16[1,4,128,128]{3,0,1,2:T(2,128)(2,1)S(1)} %copy.11), channel_id=1, source_target_pairs={{16,0},{24,8},{0,16},{8,24},{17,1},{25,9},{1,17},{9,25},{18,2},{26... | collective-permute-start | bytes 393224 | tf_op jit(solution)/shard_map/ppermute | solution.py:18
  19.4 2.3 collective-permute-start.3
  21.7 1.0 copy-start.1
  572.7 1.3 copy-start
